TPU v7x, 256 devices: a whole 4x4x8 slice. The times are simulated.
256 devices in a mesh: replica: 32 (over x, z), shard: 8 (over y, core).
Axes of the slice: x: 4, y: 4, z: 8, core: 2. Of those that a mesh axis runs over, the one named last changes fastest.
Arguments:
- grads: bfloat16 [32, 8192, 2048], P('replica', 'shard'), may hold values from -64 to 64
- errors: bfloat16 [32, 8192, 2048], P('replica', 'shard'), may hold values from -4 to 4
- q_prev: bfloat16 [32, 2048], P(None, 'shard'), may hold values from -6 to 6
- momentum: float32 [8192, 2048], P('shard', 'replica'), may hold values from -1.2 to 1.2
Outputs:
- new_errors: bfloat16 [32, 8192, 2048], P('replica', 'shard')
- new_momentum: float32 [8192, 2048], P('shard', 'replica')
- q_next: float32 [32, 2048], P(None, 'shard')
All inputs are finite; a program needn't handle non-finite values.
Results may differ from a plain program's by a relative error of at most 0.012.
Values may be sent and summed in bfloat16 or wider, within the bound.
A program may use at most 64 MiB of HBM per device.

v0:
```python
import jax
import jax.numpy as jnp
from jax import lax
from jax.sharding import PartitionSpec as P


def shards(grads, errors, q_prev, momentum):
    highest = lax.Precision.HIGHEST
    merged = grads[0].astype(jnp.float32) + errors[0].astype(jnp.float32)
    col_count = merged.shape[1]
    product = lax.dot_general(
        merged,
        lax.all_gather(q_prev, "shard", axis=1, tiled=True).astype(jnp.float32),
        (((1,), (1,)), ((), ())),
        precision=highest,
    )
    factor = lax.psum(product.astype(jnp.bfloat16), "replica").astype(jnp.float32)
    every_row = lax.all_gather(factor.astype(jnp.bfloat16), "shard", axis=0, tiled=True).astype(
        factor.dtype
    )
    gram_matrix = jnp.dot(every_row.T, every_row, precision=highest)
    lower_factor = jnp.linalg.cholesky(gram_matrix)
    ortho = jax.scipy.linalg.solve_triangular(lower_factor, factor.T, lower=True).T
    right_term = jnp.dot(ortho.T, merged, precision=highest)
    replicas = lax.axis_size("replica")
    block_width = col_count // lax.axis_size("shard")
    right_full = lax.psum(right_term, ("replica", "shard")) / replicas
    q_next = lax.dynamic_slice_in_dim(
        right_full, lax.axis_index("shard") * block_width, block_width, 1
    )
    approx = jnp.dot(ortho, right_full, precision=highest)
    new_errors = (merged - approx).astype(jnp.bfloat16)[None]
    momentum_width = momentum.shape[1]
    approx_block = lax.dynamic_slice_in_dim(
        approx, lax.axis_index("replica") * momentum_width, momentum_width, 1
    )
    new_momentum = 0.9 * momentum + approx_block
    return (new_errors, new_momentum, q_next)


def solution(mesh):
    return jax.shard_map(
        shards,
        mesh=mesh,
        in_specs=(
            P("replica", "shard", None),
            P("replica", "shard", None),
            P(None, "shard"),
            P("shard", "replica"),
        ),
        out_specs=(P("replica", "shard", None), P("shard", "replica"), P(None, "shard")),
        check_vma=False,
    )
```

profile of v0, /device:TPU:2, one launch (start us, length us, event | category | flops | bytes accessed | tf_op | source)
XLA Modules:
  0.0 478.8 jit_solution(6031099820396762904)
XLA Ops:
  7.2 0.0 all-reduce.3.cloned.1.call-start
  7.2 13.5 %all_gather.6 = bf16[32,2048]{1,0:T(8,128)(2,1)S(1)} all-gather(bf16[32,256]{1,0:T(8,128)(2,1)} %param.6), channel_id=1, replica_groups=mesh['replica'=32,'shard'=8] {'shard'}, dimensions={1}, use_global_device_ids=true | all-gather | bytes 147456 | tf_op jit(solution)/shard_map/all_gather | solution.py:13
  20.7 0.0 copy-start.2
  20.7 9.1 %fusion.6 = bf16[1024,32]{0,1:T(8,128)(2,1)} fusion(bf16[32,2048]{1,0:T(8,128)(2,1)S(1)} %all_gather.6, bf16[1,1024,2048]{2,1,0:T(8,128)(2,1)} %param.5, bf16[1,1024,2048]{2,1,0:T(8,128)(2,1)} %param.4), kind=kOutput, calls=%fused_computation.8 | convolution fusion | flops 811630592 | bytes 8585216 | tf_op jit(solution)/shard_map/dot_general | solution.py:11
  29.8 0.0 all-reduce.3.cloned.1.call-update
  29.8 0.0 all-reduce.5.cloned.1.call-start
  29.8 141.3 %all-reduce.3.cloned.1.call-done = bf16[1024,32]{0,1:T(8,128)(2,1)} async-done(((bf16[1024,32]{0,1:T(8,128)(2,1)}), bf16[1024,32]{0,1:T(8,128)(2,1)}) %all-reduce.3.cloned.1.call-update) | async-done | bytes 65552 | tf_op jit(solution)/shard_map/psum | solution.py:17
  171.2 13.8 %all_gather.7 = bf16[8192,32]{0,1:T(8,128)(2,1)S(1)} all-gather(bf16[1024,32]{0,1:T(8,128)(2,1)} %all-reduce.3.cloned.1.call-done), channel_id=1, replica_groups=mesh['replica'=32,'shard'=8] {'shard'}, dimensions={0}, use_global_device_ids=true | all-gather | bytes 589824 | tf_op jit(solution)/shard_map/all_gather | solution.py:18
  185.0 0.3 fusion.14
  185.3 0.1 copy.7
  185.4 2.9 cholesky.16
  188.3 0.6 compare_reduce_fusion
  189.0 0.7 fusion.9
  189.6 2.4 custom-call.7
  192.1 1.1 fusion.10
  193.2 8.6 %fusion = f32[32,2048]{1,0:T(8,128)} fusion(f32[32,1024]{1,0:T(8,128)S(1)} %fusion.10, bf16[1,1024,2048]{2,1,0:T(8,128)(2,1)} %param.5, bf16[1,1024,2048]{2,1,0:T(8,128)(2,1)} %param.4), kind=kOutput, calls=%fused_computation.1 | convolution fusion | flops 811597824 | bytes 8781824 | tf_op jit(solution)/shard_map/dot_general | solution.py:24
  201.7 0.0 all-reduce.5.cloned.1.call-update
  201.8 0.0 copy-done.2
  201.8 0.2 copy.8
  202.0 248.0 %all-reduce.5.cloned.1.call-done = f32[32,2048]{1,0:T(8,128)} async-done(((f32[32,2048]{1,0:T(8,128)}), f32[32,2048]{1,0:T(8,128)}) %all-reduce.5.cloned.1.call-update) | async-done | bytes 262160 | tf_op jit(solution)/shard_map/psum | solution.py:27
  450.0 0.0 copy-start
  450.0 10.0 %fusion.13 = f32[1024,2048]{1,0:T(8,128)} fusion(f32[32,1024]{1,0:T(8,128)S(1)} %fusion.10, f32[32,2048]{1,0:T(8,128)} %all-reduce.5.cloned.1.call-done), kind=kOutput, calls=%fused_computation.22 | convolution fusion | flops 805371904 | bytes 8781824 | tf_op jit(solution)/shard_map/dot_general | solution.py:31
  459.9 0.0 copy-done
  459.9 0.0 copy-start.1
  459.9 9.2 %fusion.5 = bf16[1,1024,2048]{2,1,0:T(8,128)(2,1)} fusion(f32[1024,2048]{1,0:T(8,128)} %fusion.13, bf16[1,1024,2048]{2,1,0:T(8,128)(2,1)S(1)} %copy-done, bf16[1,1024,2048]{2,1,0:T(8,128)(2,1)} %param.4), kind=kLoop, calls=%fused_computation.7 | loop fusion | flops 10485760 | bytes 20971520 | tf_op jit(solution)/shard_map/broadcast_in_dim | solution.py:32
  469.2 1.2 dynamic-slice_add_fusion
  470.4 0.9 copy.9
  471.3 0.0 copy-done.1
  471.3 0.6 constant_dynamic-slice_fusion
  (3 shorter events, 0.1 us)
Async XLA Ops:
  7.2 164.0 %all-reduce.3.cloned.1.call-start = ((), (), s32[]{:S(2)}) async-start(), calls=%async_computation | async-start | bytes 131072 | tf_op jit(solution)/shard_map/psum | solution.py:17
  20.7 181.1 %copy-start.2 = (f32[1024,64]{0,1:T(8,128)S(1)}, f32[1024,64]{0,1:T(8,128)}, u32[]{:S(2)}) copy-start(f32[1024,64]{0,1:T(8,128)} %param.7) | copy-start | bytes 786436
  29.8 420.2 %all-reduce.5.cloned.1.call-start = ((), (), s32[]{:S(2)}) async-start(), calls=%async_computation.1 | async-start | bytes 524288 | tf_op jit(solution)/shard_map/psum | solution.py:27
  450.0 10.0 %copy-start = (bf16[1,1024,2048]{2,1,0:T(8,128)(2,1)S(1)}, bf16[1,1024,2048]{2,1,0:T(8,128)(2,1)}, u32[]{:S(2)}) copy-start(bf16[1,1024,2048]{2,1,0:T(8,128)(2,1)} %param.5) | copy-start | bytes 12582916
  459.9 11.4 %copy-start.1 = (f32[32,2048]{1,0:T(8,128)S(1)}, f32[32,2048]{1,0:T(8,128)}, u32[]{:S(2)}) copy-start(f32[32,2048]{1,0:T(8,128)} %all-reduce.5.cloned.1.call-done) | copy-start | bytes 786436
Sparse Core Ops, SparseCore 0:
  29.9 141.2 all-reduce.2
  201.9 248.0 all-reduce.4
where the time goes:
time: 479 us
  waiting for transfers between devices  389 us (81%)
  matrix products  29 us (6%)
  blocking collectives  27.3 us (6%)
  other arithmetic  17.2 us (4%)
  between operations  14.1 us (3%)
    psum x1, waiting for transfers between devices, shards(): right_full = lax.psum(right_term, ('replica', 'shard')) / replicas  248 us
    psum x1, waiting for transfers between devices, shards(): lax.psum(product.astype(jnp.bfloat16), 'replica').astype(jnp.float32)  141 us
    all_gather x1, blocking collectives, shards(): lax.all_gather(factor.astype(jnp.bfloat16), 'shard', axis=0, tiled=True)  13.8 us
    all_gather x1, blocking collectives, shards(): lax.all_gather(q_prev, 'shard', axis=1, tiled=True).astype(jnp.float32)  13.5 us
    dot_general x1, matrix products, shards(): approx = jnp.dot(ortho, right_full, precision=highest)  9.98 us
  transfers between devices with their start and end apart: 2, of which 2 were waited for; matrix products, arithmetic and copies ran while one was open for 0% of the time, Pallas kernels for 0%

commit v1 on v0

--- a/solution.py
+++ b/solution.py
@@ -2,6 +2,10 @@
 import jax.numpy as jnp
 from jax import lax
 from jax.sharding import PartitionSpec as P
+
+
+def supply_all_layers_all(field, device_axis, mesh_dim):
+    return jax.lax.psum(jax.lax.psum(field, axis_name=mesh_dim), axis_name=device_axis)
 
 
 def shards(grads, errors, q_prev, momentum):
@@ -24,7 +28,7 @@
     right_term = jnp.dot(ortho.T, merged, precision=highest)
     replicas = lax.axis_size("replica")
     block_width = col_count // lax.axis_size("shard")
-    right_full = lax.psum(right_term, ("replica", "shard")) / replicas
+    right_full = supply_all_layers_all(right_term, "shard", "replica") / replicas
     q_next = lax.dynamic_slice_in_dim(
         right_full, lax.axis_index("shard") * block_width, block_width, 1
     )

time: 479 us -> 437 us (0.912)
  waiting for transfers between devices: 389 us -> 347 us
    psum x1 -> x2, waiting for transfers between devices: 248 us -> 206 us  [the longest x1 141 us: supply_all_layers_all(): jax.lax.psum(field, axis_name=mesh_dim)]
  transfers between devices with their start and end apart: 2 -> 3, of which waited for: 2 -> 3; matrix products, arithmetic and copies ran while one was open for 0% -> 0% of each run, Pallas kernels for 0% -> 0%
where the time goes in v1:
time: 437 us; the launch traced here: 436 us
  waiting for transfers between devices  347 us (79%)
  matrix products  29 us (7%)
  blocking collectives  27.1 us (6%)
  other arithmetic  17.2 us (4%)
  between operations  13.8 us (3%)
    psum x1, waiting for transfers between devices, shards(): lax.psum(product.astype(jnp.bfloat16), 'replica').astype(jnp.float32)  141 us
    psum x1, waiting for transfers between devices, supply_all_layers_all(): jax.lax.psum(field, axis_name=mesh_dim)  141 us
    psum x1, waiting for transfers between devices, supply_all_layers_all(): jax.lax.psum(jax.lax.psum(field, axis_name=mesh_dim), axis_name=device_axis)  65.2 us
    all_gather x1, blocking collectives, shards(): lax.all_gather(factor.astype(jnp.bfloat16), 'shard', axis=0, tiled=True)  13.6 us
    all_gather x1, blocking collectives, shards(): lax.all_gather(q_prev, 'shard', axis=1, tiled=True).astype(jnp.float32)  13.5 us
    dot_general x1, matrix products, shards(): approx = jnp.dot(ortho, right_full, precision=highest)  9.98 us
    broadcast_in_dim x1, other arithmetic, shards(): new_errors = (merged - approx).astype(jnp.bfloat16)[None]  9.22 us
    dot_general x1, matrix products, shards(): lax.dot_general(merged, lax.all_gather(q_prev, 'shard', axis=1, tiled=Tru...  9.05 us
  transfers between devices with their start and end apart: 3, of which 3 were waited for; matrix products, arithmetic and copies ran while one was open for 0% of the time, Pallas kernels for 0%

profile of v1, /device:TPU:2, one launch (start us, length us, event | category | flops | bytes accessed | tf_op | source)
XLA Modules:
  0.0 436.4 jit_solution(10297928092489798604)
XLA Ops:
  7.2 0.0 all-reduce.4.cloned.1.call-start
  7.2 13.5 %all_gather.6 = bf16[32,2048]{1,0:T(8,128)(2,1)S(1)} all-gather(bf16[32,256]{1,0:T(8,128)(2,1)} %param.6), channel_id=1, replica_groups=mesh['replica'=32,'shard'=8] {'shard'}, dimensions={1}, use_global_device_ids=true | all-gather | bytes 147456 | tf_op jit(solution)/shard_map/all_gather | solution.py:17
  20.7 0.0 copy-start.2
  20.7 9.1 %fusion.6 = bf16[1024,32]{0,1:T(8,128)(2,1)} fusion(bf16[32,2048]{1,0:T(8,128)(2,1)S(1)} %all_gather.6, bf16[1,1024,2048]{2,1,0:T(8,128)(2,1)} %param.5, bf16[1,1024,2048]{2,1,0:T(8,128)(2,1)} %param.4), kind=kOutput, calls=%fused_computation.8 | convolution fusion | flops 811630592 | bytes 8585216 | tf_op jit(solution)/shard_map/dot_general | solution.py:15
  29.8 0.0 all-reduce.4.cloned.1.call-update
  29.8 0.0 all-reduce.6.cloned.1.call-start
  29.8 141.3 %all-reduce.4.cloned.1.call-done = bf16[1024,32]{0,1:T(8,128)(2,1)} async-done(((bf16[1024,32]{0,1:T(8,128)(2,1)}), bf16[1024,32]{0,1:T(8,128)(2,1)}) %all-reduce.4.cloned.1.call-update) | async-done | bytes 65552 | tf_op jit(solution)/shard_map/psum | solution.py:21
  171.2 13.6 %all_gather.7 = bf16[8192,32]{0,1:T(8,128)(2,1)S(1)} all-gather(bf16[1024,32]{0,1:T(8,128)(2,1)} %all-reduce.4.cloned.1.call-done), channel_id=1, replica_groups=mesh['replica'=32,'shard'=8] {'shard'}, dimensions={0}, use_global_device_ids=true | all-gather | bytes 589824 | tf_op jit(solution)/shard_map/all_gather | solution.py:22
  184.8 0.3 fusion.14
  185.1 0.1 copy.7
  185.2 2.9 cholesky.16
  188.1 0.6 compare_reduce_fusion
  188.8 0.7 fusion.9
  189.4 2.4 custom-call.7
  191.9 1.1 fusion.10
  193.0 8.6 %fusion = f32[32,2048]{1,0:T(8,128)} fusion(f32[32,1024]{1,0:T(8,128)S(1)} %fusion.10, bf16[1,1024,2048]{2,1,0:T(8,128)(2,1)} %param.5, bf16[1,1024,2048]{2,1,0:T(8,128)(2,1)} %param.4), kind=kOutput, calls=%fused_computation.1 | convolution fusion | flops 811597824 | bytes 8781824 | tf_op jit(solution)/shard_map/dot_general | solution.py:28
  201.6 0.0 all-reduce.6.cloned.1.call-update
  201.6 0.2 all-reduce.8.cloned.1.call-start
  201.8 140.6 %all-reduce.6.cloned.1.call-done = f32[32,2048]{1,0:T(8,128)} async-done(((f32[32,2048]{1,0:T(8,128)}), f32[32,2048]{1,0:T(8,128)}) %all-reduce.6.cloned.1.call-update) | async-done | bytes 262160 | tf_op jit(solution)/shard_map/psum | solution.py:8
  342.4 0.0 all-reduce.8.cloned.1.call-update
  342.4 0.0 copy-done.2
  342.4 0.2 copy.8
  342.6 65.2 %all-reduce.8.cloned.1.call-done = f32[32,2048]{1,0:T(8,128)} async-done(((f32[32,2048]{1,0:T(8,128)}), f32[32,2048]{1,0:T(8,128)}) %all-reduce.8.cloned.1.call-update) | async-done | bytes 262160 | tf_op jit(solution)/shard_map/psum | solution.py:8
  407.8 0.0 copy-start
  407.8 10.0 %fusion.13 = f32[1024,2048]{1,0:T(8,128)} fusion(f32[32,1024]{1,0:T(8,128)S(1)} %fusion.10, f32[32,2048]{1,0:T(8,128)} %all-reduce.8.cloned.1.call-done), kind=kOutput, calls=%fused_computation.22 | convolution fusion | flops 805371904 | bytes 8781824 | tf_op jit(solution)/shard_map/dot_general | solution.py:35
  417.8 0.0 copy-done
  417.8 0.0 copy-start.1
  417.8 9.2 %fusion.5 = bf16[1,1024,2048]{2,1,0:T(8,128)(2,1)} fusion(f32[1024,2048]{1,0:T(8,128)} %fusion.13, bf16[1,1024,2048]{2,1,0:T(8,128)(2,1)S(1)} %copy-done, bf16[1,1024,2048]{2,1,0:T(8,128)(2,1)} %param.4), kind=kLoop, calls=%fused_computation.7 | loop fusion | flops 10485760 | bytes 20971520 | tf_op jit(solution)/shard_map/broadcast_in_dim | solution.py:36
  427.1 1.2 dynamic-slice_add_fusion
  428.3 0.9 copy.9
  429.2 0.0 copy-done.1
  429.2 0.6 constant_dynamic-slice_fusion
  (3 shorter events, 0.1 us)
Async XLA Ops:
  7.2 164.0 %all-reduce.4.cloned.1.call-start = ((), (), s32[]{:S(2)}) async-start(), calls=%async_computation | async-start | bytes 131072 | tf_op jit(solution)/shard_map/psum | solution.py:21
  20.7 321.7 %copy-start.2 = (f32[1024,64]{0,1:T(8,128)S(1)}, f32[1024,64]{0,1:T(8,128)}, u32[]{:S(2)}) copy-start(f32[1024,64]{0,1:T(8,128)} %param.7) | copy-start | bytes 786436
  29.8 312.6 %all-reduce.6.cloned.1.call-start = ((), (), s32[]{:S(2)}) async-start(), calls=%async_computation.1 | async-start | bytes 524288 | tf_op jit(solution)/shard_map/psum | solution.py:8
  201.6 206.3 %all-reduce.8.cloned.1.call-start = ((), (), s32[]{:S(2)}) async-start(), calls=%async_computation.2 | async-start | bytes 524288 | tf_op jit(solution)/shard_map/psum | solution.py:8
  407.8 10.0 %copy-start = (bf16[1,1024,2048]{2,1,0:T(8,128)(2,1)S(1)}, bf16[1,1024,2048]{2,1,0:T(8,128)(2,1)}, u32[]{:S(2)}) copy-start(bf16[1,1024,2048]{2,1,0:T(8,128)(2,1)} %param.5) | copy-start | bytes 12582916
  417.8 11.4 %copy-start.1 = (f32[32,2048]{1,0:T(8,128)S(1)}, f32[32,2048]{1,0:T(8,128)}, u32[]{:S(2)}) copy-start(f32[32,2048]{1,0:T(8,128)} %all-reduce.8.cloned.1.call-done) | copy-start | bytes 786436
Sparse Core Ops, SparseCore 0:
  29.9 141.2 all-reduce.3
  201.7 140.6 all-reduce.5
  344.7 63.1 all-reduce.7
